TPU v7x, 32 devices: a whole 2x2x4 slice. The times are simulated.
32 devices in a mesh: elem: 8 (over z, y), blk: 4 (over x, core).
Axes of the slice: x: 2, y: 2, z: 4, core: 2. Of those that a mesh axis runs over, the one named last changes fastest.
Arguments:
- tangent_in: float32 [4, 64, 16384], P(None, None, ('elem', 'blk')), may hold values from -6 to 6
- forward_state: float32 [4, 64, 16384], P(None, None, ('elem', 'blk')), may hold values from -6 to 6
- adjoint_in: float32 [4, 64, 16384], P(None, None, ('elem', 'blk')), may hold values from -6 to 6
- bulk_modulus: float32 [16384], P(('elem', 'blk')), may hold values from 0.5 to 2
- param_step: float32 [4096], P(('elem', 'blk')), may hold values from -6 to 6
- neighbours: int32 [6, 16384], P(None, ('elem', 'blk')), may hold values from 0 to 767, as said below
- export_slots: int32 [2, 8192], P(None, ('elem', 'blk')), may hold values from 0 to 511, as said below
- param_map: int32 [4096], P(('elem', 'blk')), may hold values from 0 to 4095, as said below
Outputs:
- tangent_out: float32 [4, 64, 16384], P(None, None, ('elem', 'blk'))
- adjoint_out: float32 [4, 64, 16384], P(None, None, ('elem', 'blk'))
- hvp: float32 [4096], P(('elem', 'blk'))
Inputs may be any that keep to these rules, and one draw needn't show every extreme that they name: Each device's elements form a slab of 16 x 16 x 2 hexahedra of a periodic box, stored in a permuted order; the slabs are stacked along z in the order of elem+blk. Entries at or above 512 occur only for the faces -z and +z and name ghost slot entry - 512; face neighbours are mutual. `export_slots`: row 0 lists the elements whose +z face borders the next device, row 1 those whose -z face borders the previous device, in the ghost slot order that the receiving device's neighbours use. `param_map`: the block of device d names a parameter cell owned by a device whose index along elem+blk differs from d by at most 2, cyclically; a device owns cells d * 128 to (d + 1) * 128 - 1; every device has blocks whose owner lies exactly 2 below and exactly 2 above.
All inputs are finite; a program needn't handle non-finite values.
Results may differ from a plain program's by a relative error of at most 0.0001.
Values sent between devices are 32-bit elements; how exact they have to be, the bound alone decides.
A program may use at most 64 MiB of HBM per device.

v0:
```python
import functools

import jax
import jax.numpy as jnp
import ml_dtypes
import numpy as np
from jax import lax
from jax.experimental import pallas as pl
from jax.experimental.pallas import tpu as pltpu
from jax.sharding import PartitionSpec as P

BLOCK = 4
REACH = 2
LIFT = 6.0
DT = 0.1
HALF = 0.5 * LIFT
INPUTS = 19
ORDER = (6, 0, 1, 4, 5, 14, 15, 8, 9, 10, 11, 7, 3, 17, 2, 18, 16, 12, 13)
MESH = pl.DeviceIdType.MESH
BF16 = jnp.bfloat16
F32 = jnp.float32


def split_np(matrix):
    high = matrix.astype(np.float32).astype(ml_dtypes.bfloat16)
    low = (matrix - high.astype(np.float64)).astype(np.float32).astype(ml_dtypes.bfloat16)
    return high, low


def tables():
    points = np.array([-1.0, -1.0 / np.sqrt(5.0), 1.0 / np.sqrt(5.0), 1.0])
    one = np.zeros((4, 4))
    for i in range(4):
        for j in range(4):
            if i != j:
                top = np.prod([points[i] - points[k] for k in range(4) if k != i and k != j])
                one[i, j] = top / np.prod([points[j] - points[k] for k in range(4) if k != j])
        one[i, i] = np.sum([1.0 / (points[i] - points[k]) for k in range(4) if k != i])
    eye = np.eye(4)
    deriv = [
        np.kron(np.eye(16), one),
        np.kron(eye, np.kron(one, eye)),
        np.kron(one, np.eye(16)),
    ]
    node = np.arange(64)
    place = [node % 4, node // 4 % 4, node // 16]
    faces = [np.flatnonzero(place[f // 2] == 3 * (f % 2)) for f in range(6)]
    sel = np.zeros((6, 16, 64))
    for f in range(6):
        sel[f, np.arange(16), faces[f]] = 1.0
    count = sel.sum((0, 1))
    local = []
    for d in range(3):
        ends = np.diag(sel[2 * d + 1].sum(0) - sel[2 * d].sum(0))
        local.append(-deriv[d] + HALF * ends)
    weights = np.array([1.0 / 6.0, 5.0 / 6.0, 5.0 / 6.0, 1.0 / 6.0])
    mass = np.kron(weights, np.kron(weights, weights))

    own = np.zeros((256, 256))
    for d in range(3):
        rows = slice(64 + 64 * d, 128 + 64 * d)
        own[:64, rows] = local[d]
        own[rows, :64] = local[d]
    sens = np.concatenate(local, 1)

    sel_t = np.zeros((256, 256))
    sel_f = np.zeros((64, 128))
    sel_a = np.zeros((320, 320))
    lift_t = np.zeros((320, 256))
    lift_s = np.zeros((64, 64))
    lift_a = np.zeros((256, 320))
    for f in range(4):
        d = f // 2
        s = 2.0 * (f % 2) - 1.0
        far = sel[f ^ 1]
        near = sel[f].T
        for k in range(4):
            sel_t[64 * f + 16 * k : 64 * f + 16 * k + 16, 64 * k : 64 * k + 64] = far
        for k in range(5):
            sel_a[80 * f + 16 * k : 80 * f + 16 * k + 16, 64 * k : 64 * k + 64] = far
        sel_f[16 * f : 16 * f + 16, 64 * d : 64 * d + 64] = far
        lift_s[:, 16 * f : 16 * f + 16] = -HALF * s * near
        at = 64 * f
        lift_t[0:64, at : at + 16] += HALF * near
        lift_t[64:128, at + 16 + 16 * d : at + 32 + 16 * d] += -HALF * s * near
        for k in range(3):
            lift_t[128 + 64 * k : 192 + 64 * k, at + 16 + 16 * k : at + 32 + 16 * k] += HALF * near
        lift_t[128 + 64 * d : 192 + 64 * d, at : at + 16] += -HALF * s * near
        at = 80 * f
        lift_a[0:64, at + 64 : at + 80] += HALF * near
        lift_a[0:64, at + 16 + 16 * d : at + 32 + 16 * d] += HALF * s * near
        for k in range(3):
            lift_a[64 + 64 * k : 128 + 64 * k, at + 16 + 16 * k : at + 32 + 16 * k] += HALF * near
        lift_a[64 + 64 * d : 128 + 64 * d, at : at + 16] += HALF * s * near

    own_h, own_l = split_np(own)
    adj_h, adj_l = split_np(own.T)
    sen_h, sen_l = split_np(sens)
    wide = np.zeros((320, 256), own_h.dtype)
    wide[64:] = own_h
    lift_t = lift_t.astype(own_h.dtype)
    lift_s = lift_s.astype(own_h.dtype)
    lift_a = lift_a.astype(own_h.dtype)
    return [
        np.concatenate([wide, wide, lift_t, lift_t], 1),
        own_l,
        np.concatenate([sen_h, sen_h, lift_s, lift_s], 1),
        sen_l,
        np.concatenate([adj_h, adj_h, lift_a, lift_a], 1),
        adj_l,
        sel_t.astype(own_h.dtype),
        sel_f.astype(own_h.dtype),
        sel_a.astype(own_h.dtype),
        np.repeat((DT * HALF * count)[:, None], 128, 1).astype(np.float32),
        np.repeat((2.0 * DT * mass)[:, None], 128, 1).astype(np.float32),
    ]


def dot(a, b):
    return jnp.dot(a, b, preferred_element_type=F32)


def dot_nt(a, b):
    return lax.dot_general(a, b, (((1,), (1,)), ((), ())), preferred_element_type=F32)


def split(value):
    high = value.astype(BF16)
    return high, (value - high.astype(F32)).astype(BF16)


def stack(value):
    return jnp.concatenate(split(value), 0)


def hot(row, rows, base=0):
    width = row.shape[1]
    at = lax.broadcasted_iota(jnp.int32, (rows, width), 0) + base
    return jnp.where(at == row, 1.0, 0.0).astype(BF16)


def wide(column):
    return jnp.concatenate([column] * 4, 1)


def kernel(
    devices,
    n_blk,
    *refs,
):
    sources, refs = refs[:INPUTS], refs[INPUTS:]
    t_out, a_out, h_out = refs[:3]
    refs = refs[3:]
    held, refs = refs[:INPUTS], refs[INPUTS:]
    (
    isem,
    hots,
    ghots,
    exps,
    x1,
    xs,
    x2,
    wz,
    send1,
    recv1,
    send2,
    recv2,
    table,
    psend,
    hsend,
    hrecv,
    ssem1,
    rsem1,
    ssem2,
    rsem2,
    pssem,
    prsem,
    hssem,
    hrsem,
    ) = refs
    (
        q_ref,
        f_ref,
        a_ref,
        k_ref,
        ps_ref,
        nb_ref,
        ex_ref,
        pm_ref,
        main_m,
        main_l,
        sens_m,
        sens_l,
        adj_m,
        adj_l,
        sel_t,
        sel_f,
        sel_a,
        count_ref,
        mass_ref,
    ) = held
    loads = [
        pltpu.make_async_copy(sources[i], held[i], isem.at[i]) for i in range(INPUTS)
    ]
    for i in ORDER:
        loads[i].start()

    def need(*which):
        for i in which:
            loads[i].wait()

    me = lax.axis_index("elem") * n_blk + lax.axis_index("blk")

    def device(step):
        other = lax.rem(me + step + devices, devices)
        return (other // n_blk, lax.rem(other, n_blk))

    steps = [s for s in range(-REACH, REACH + 1) if s]
    barrier = pltpu.get_barrier_semaphore()
    for s in steps:
        pl.semaphore_signal(barrier, inc=1, device_id=device(s), device_id_type=MESH)

    def remote(src, dst, ssem, rsem, step):
        return pltpu.make_async_remote_copy(
            src_ref=src,
            dst_ref=dst,
            send_sem=ssem,
            recv_sem=rsem,
            device_id=device(step),
            device_id_type=MESH,
        )

    def z_trace(refs, top):
        at = 48 if top else 0
        return jnp.concatenate([r[o + at : o + at + 16, :] for r, o in refs], 0)

    fields = [(q_ref, 0), (q_ref, 64), (q_ref, 128), (q_ref, 192), (f_ref, 192)]
    need(6, 0, 1, 4)
    psend[...] = jnp.broadcast_to(ps_ref[...], psend.shape)
    for way in range(2):
        exps[way] = hot(ex_ref[way : way + 1, :], 512)
        both = stack(z_trace(fields, way == 0))
        x2[way * 160 : way * 160 + 160, :] = both
        gathered = dot(both, exps[way])
        send1[way] = gathered[:80] + gathered[80:]
    pl.semaphore_wait(barrier, len(steps))
    copies1 = []
    for way in range(2):
        copy = remote(send1.at[way], recv1.at[way], ssem1.at[way], rsem1.at[way], 1 - 2 * way)
        copy.start()
        copies1.append(copy)
    pcopies = []
    for i, s in enumerate(steps):
        copy = remote(psend, table.at[REACH - s], pssem.at[i], prsem.at[REACH - s], s)
        copy.start()
        pcopies.append(copy)

    need(5)
    for f in range(6):
        hots[f] = hot(nb_ref[f : f + 1, :], 512)
    for way in range(2):
        ghots[way] = hot(nb_ref[4 + way : 5 + way, :], 256, 512)
    q_h, q_l = split(q_ref[...])
    x1[0:256, :] = q_h
    x1[256:512, :] = q_l
    u_h, u_l = split(f_ref[64:256, :])
    xs[0:192, :] = u_h
    xs[192:384, :] = u_l
    for way in range(2):
        inside = dot(x2[way * 160 : way * 160 + 160, :], hots[4 + way])
        wz[way] = inside[:80] + inside[80:]
    need(14, 15)
    t_h = dot(sel_t[...], x1[0:256, :]).astype(BF16)
    t_l = dot(sel_t[...], x1[256:512, :]).astype(BF16)
    tf_h = dot(sel_f[...], xs[0:128, :]).astype(BF16)
    tf_l = dot(sel_f[...], xs[192:320, :]).astype(BF16)
    for f in range(4):
        big = slice(64 * f, 64 * f + 64)
        small = slice(16 * f, 16 * f + 16)
        lhs = jnp.concatenate([t_h[big], t_l[big], tf_h[small], tf_l[small]], 0)
        far = dot(lhs, hots[f]).astype(BF16)
        x1[512 + 64 * f : 576 + 64 * f, :] = far[0:64]
        x1[768 + 64 * f : 832 + 64 * f, :] = far[64:128]
        xs[384 + 16 * f : 400 + 16 * f, :] = far[128:144]
        xs[448 + 16 * f : 464 + 16 * f, :] = far[144:160]
    need(8, 9, 10, 11, 3, 7)
    main = dot(main_m[...], x1[...])
    main_low = dot(main_l[...], x1[0:256, :])
    sense = dot(sens_m[...], xs[...]) + dot(sens_l[...], xs[0:192, :])
    bulk = jnp.broadcast_to(k_ref[...], (64, 512))

    pm = pm_ref[...]
    cells = ps_ref.shape[1]
    owner = pm // cells
    cell = pm - owner * cells
    where = owner - me + REACH
    where = jnp.where(where < 0, where + devices, where)
    where = jnp.where(where >= devices, where - devices, where)
    cell_hot = hot(cell, cells)
    blocks = pm.shape[1]
    repeat = jnp.where(
        lax.broadcasted_iota(jnp.int32, (blocks, 512), 1) // BLOCK
        == lax.broadcasted_iota(jnp.int32, (blocks, 512), 0),
        1.0,
        0.0,
    ).astype(BF16)
    for copy in pcopies:
        copy.wait()
    table[REACH] = psend[...]
    span = 2 * REACH + 1
    picked = dot(stack(table[...].reshape(8 * span, cells)), cell_hot)
    picked = picked[: 8 * span] + picked[8 * span :]
    block_step = jnp.zeros((8, blocks), F32)
    for o in range(span):
        block_step = jnp.where(where == o, picked[8 * o : 8 * o + 8], block_step)
    spread = dot(stack(block_step), repeat)
    step = jnp.concatenate([spread[:8] + spread[8:]] * 8, 0)

    for way in range(2):
        copies1[way].wait()
        outside = dot(stack(recv1[way]), ghots[way])
        wz[way] = wz[way] + outside[:80] + outside[80:]

    low, high = wz[0], wz[1]

    def z_add(value, first, last):
        return jnp.concatenate([value[0:16] + first, value[16:48], value[48:64] + last], 0)

    sense = z_add(sense, HALF * low[64:80], -HALF * high[64:80])
    r_a = z_add(main[0:64], HALF * low[0:16], HALF * high[0:16])
    r_b = z_add(main[64:128] + main_low[0:64], HALF * low[48:64], -HALF * high[48:64])
    r_b = r_b + 2.0 * step * sense
    need(17, 2)
    count = wide(count_ref[...])
    q = q_ref[0:64, :]
    new = q - count * q + DT * (r_a + bulk * r_b)
    t_out[0:64, :] = new
    lam = a_ref[0:64, :] + new
    lam_p = lam
    k_lam = bulk * lam
    a_out[0:64, :] = lam
    k_h, k_l = split(k_lam)
    p_h, p_l = split(lam)
    x2[0:64, :] = k_h
    x2[320:384, :] = k_l
    x2[256:320, :] = p_h
    x2[576:640, :] = p_l
    ztop = [k_lam[48:64]]
    zbot = [k_lam[0:16]]
    for k in range(3):
        at = 64 + 64 * k
        first, last = low[16 + 16 * k : 32 + 16 * k], high[16 + 16 * k : 32 + 16 * k]
        if k == 2:
            first = first + low[0:16]
            last = last - high[0:16]
        r_u = z_add(main[64 + at : 128 + at] + main_low[at : at + 64], HALF * first, HALF * last)
        q = q_ref[at : at + 64, :]
        new = q - count * q + DT * r_u
        t_out[at : at + 64, :] = new
        lam = a_ref[at : at + 64, :] + new
        a_out[at : at + 64, :] = lam
        l_h, l_l = split(lam)
        x2[at : at + 64, :] = l_h
        x2[320 + at : 384 + at, :] = l_l
        ztop.append(lam[48:64])
        zbot.append(lam[0:16])
    ztop.append(lam_p[48:64])
    zbot.append(lam_p[0:16])

    copies2 = []
    zboth = []
    for way in range(2):
        both = stack(jnp.concatenate(ztop if way == 0 else zbot, 0))
        zboth.append(both)
        gathered = dot(both, exps[way])
        send2[way] = gathered[:80] + gathered[80:]
        copy = remote(send2.at[way], recv2.at[way], ssem2.at[way], rsem2.at[way], 1 - 2 * way)
        copy.start()
        copies2.append(copy)

    need(18)
    term = bulk * wide(mass_ref[...]) * lam_p * sense
    total = term[0:8]
    for i in range(1, 8):
        total = total + term[8 * i : 8 * i + 8]
    block_term = dot_nt(stack(total), repeat)
    block_term = block_term[:8] + block_term[8:]
    parts = jnp.concatenate([jnp.where(where == o, block_term, 0.0) for o in range(span)], 0)
    owned = dot_nt(stack(parts), cell_hot)
    owned = owned[: 8 * span] + owned[8 * span :]
    hsend[...] = owned.reshape(span, 8, cells)
    hcopies = []
    for i, s in enumerate(steps):
        copy = remote(hsend.at[REACH + s], hrecv.at[i], hssem.at[i], hrsem.at[i], s)
        copy.start()
        hcopies.append(copy)

    need(16, 12, 13)
    for way in range(2):
        inside = dot(zboth[way], hots[4 + way])
        wz[way] = inside[:80] + inside[80:]
    t_h = dot(sel_a[...], x2[0:320, :]).astype(BF16)
    t_l = dot(sel_a[...], x2[320:640, :]).astype(BF16)
    x2[256:512, :] = x2[320:576, :]
    for f in range(4):
        rows = slice(80 * f, 80 * f + 80)
        far = dot(jnp.concatenate([t_h[rows], t_l[rows]], 0), hots[f]).astype(BF16)
        x2[512 + 80 * f : 592 + 80 * f, :] = far[0:80]
        x2[832 + 80 * f : 912 + 80 * f, :] = far[80:160]
    result = dot(adj_m[...], x2[...]) + dot(adj_l[...], x2[0:256, :])

    for way in range(2):
        copies2[way].wait()
        outside = dot(stack(recv2[way]), ghots[way])
        wz[way] = wz[way] + outside[:80] + outside[80:]
    low, high = wz[0], wz[1]
    for k in range(4):
        at = 64 * k
        if k == 0:
            first = low[64:80] - low[48:64]
            last = high[64:80] + high[48:64]
        else:
            first, last = low[16 * k : 16 * k + 16], high[16 * k : 16 * k + 16]
            if k == 3:
                first = first - low[0:16]
                last = last + high[0:16]
        r = z_add(result[at : at + 64], HALF * first, HALF * last)
        lam = a_out[at : at + 64, :]
        a_out[at : at + 64, :] = lam - count * lam + DT * r

    for copy in hcopies:
        copy.wait()
    total = hsend[REACH]
    for i in range(len(steps)):
        total = total + hrecv[i]
    h_out[...] = jnp.sum(total, 0, keepdims=True)


def solution(mesh):
    axes = ("elem", "blk")
    devices = mesh.shape["elem"] * mesh.shape["blk"]
    n_blk = mesh.shape["blk"]
    consts = tables()

    def local(tangent, forward, adjoint, bulk, param, neighbours, exports, param_map):
        hbm = pl.BlockSpec(memory_space=pltpu.HBM)
        vmem = pl.BlockSpec(memory_space=pltpu.VMEM)
        args = [
            tangent.reshape(256, 512),
            forward.reshape(256, 512),
            adjoint.reshape(256, 512),
            bulk.reshape(1, 512),
            param.reshape(1, -1),
            neighbours,
            exports,
            param_map.reshape(1, -1),
            *[jnp.asarray(c) for c in consts],
        ]
        span = 2 * REACH + 1
        cells = param.shape[0]
        dma = pltpu.SemaphoreType.DMA
        t_out, a_out, h_out = pl.pallas_call(
            functools.partial(kernel, devices, n_blk),
            out_shape=(
                jax.ShapeDtypeStruct((256, 512), F32),
                jax.ShapeDtypeStruct((256, 512), F32),
                jax.ShapeDtypeStruct((1, cells), F32),
            ),
            in_specs=[hbm] * INPUTS,
            out_specs=(vmem,) * 3,
            scratch_shapes=[pltpu.VMEM(a.shape, a.dtype) for a in args]
            + [
                dma((INPUTS,)),
                pltpu.VMEM((6, 512, 512), BF16),
                pltpu.VMEM((2, 256, 512), BF16),
                pltpu.VMEM((2, 512, 256), BF16),
                pltpu.VMEM((1024, 512), BF16),
                pltpu.VMEM((512, 512), BF16),
                pltpu.VMEM((1152, 512), BF16),
                pltpu.VMEM((2, 80, 512), F32),
                pltpu.VMEM((2, 80, 256), F32),
                pltpu.VMEM((2, 80, 256), F32),
                pltpu.VMEM((2, 80, 256), F32),
                pltpu.VMEM((2, 80, 256), F32),
                pltpu.VMEM((span, 8, cells), F32),
                pltpu.VMEM((8, cells), F32),
                pltpu.VMEM((span, 8, cells), F32),
                pltpu.VMEM((2 * REACH, 8, cells), F32),
                dma((2,)),
                dma((2,)),
                dma((2,)),
                dma((2,)),
                dma((2 * REACH,)),
                dma((span,)),
                dma((2 * REACH,)),
                dma((2 * REACH,)),
            ],
            compiler_params=pltpu.CompilerParams(
                collective_id=0, has_side_effects=True, vmem_limit_bytes=62 * 2**20
            ),
        )(*args)
        return (
            t_out.reshape(4, 64, 512),
            a_out.reshape(4, 64, 512),
            h_out.reshape(cells),
        )

    whole = P(None, None, axes)
    row = P(axes)
    return jax.shard_map(
        local,
        mesh=mesh,
        in_specs=(whole, whole, whole, row, row, P(None, axes), P(None, axes), row),
        out_specs=(whole, whole, row),
        check_vma=False,
    )
```

profile of v0, /device:TPU:0, one launch (start us, length us, event | category | flops | bytes accessed | tf_op | source)
XLA Modules:
  0.0 23.8 jit_solution(14105877658372578459)
XLA Ops:
  0.6 19.9 %shard_map.202 = (f32[256,512]{1,0:T(8,128)}, f32[256,512]{1,0:T(8,128)}, f32[1,128]{1,0:T(1,128)}) custom-call(f32[256,512]{1,0:T(8,128)} %bitcast.9, f32[256,512]{1,0:T(8,128)} %bitcast.10, f32[256,512]{1,0:T(8,128)} %bitcast.11, f32[1,512]{1,0:T(1,128)} %bitcast.14, f32[1,128]{1,0:T(1,128)} %bitcast.15, s32[6,512]{1,0:T(8,128)} %refs_5_.1, ...), custom_call_target="tpu_custom_call" | custom-call | tf_op jit(solution)/shard_map/pallas_call | solution.py:462
  20.6 0.0 copy-start
  20.6 1.9 %copy.25 = f32[4,64,512]{2,1,0:T(8,128)} copy(f32[4,64,512]{2,1,0:T(8,128)} %bitcast.13) | data formatting | bytes 1048576
  22.5 0.0 copy-done
  22.5 0.0 copy-start.1
  22.5 0.8 %copy.26 = f32[4,64,512]{2,1,0:T(8,128)} copy(f32[4,64,512]{2,1,0:T(8,128)S(1)} %bitcast.12) | data formatting | bytes 1048576
  23.3 0.0 copy-done.1
  23.3 0.5 %copy.27 = f32[128]{0:T(128)} copy(f32[128]{0:T(128)S(1)} %bitcast.17) | data formatting | bytes 1024
Async XLA Ops:
  20.6 1.9 %copy-start = (f32[256,512]{1,0:T(8,128)S(1)}, f32[256,512]{1,0:T(8,128)}, u32[]{:S(2)}) copy-start(f32[256,512]{1,0:T(8,128)} %get-tuple-element.7) | copy-start | bytes 1572868
  22.5 0.8 %copy-start.1 = (f32[1,128]{1,0:T(1,128)S(1)}, f32[1,128]{1,0:T(1,128)}, u32[]{:S(2)}) copy-start(f32[1,128]{1,0:T(1,128)} %get-tuple-element.8) | copy-start | bytes 1540
where the time goes:
time: 24 us; the launch traced here: 23.8 us
  Pallas kernels  19.9 us (83%)
  local copies, waits for them, and re-layouts  3.24 us (14%)
  between operations  0.65 us (3%)
    pallas_call x1, Pallas kernels, local(): pl.pallas_call(functools.partial(kernel, devices, n_blk), out_shape=(jax....  19.9 us
    unnamed x7, local copies, waits for them, and re-layouts  3.24 us

commit v1 on v0

--- a/solution.py
+++ b/solution.py
@@ -15,7 +15,8 @@
 DT = 0.1
 HALF = 0.5 * LIFT
 INPUTS = 19
-ORDER = (6, 0, 1, 4, 5, 14, 15, 8, 9, 10, 11, 7, 3, 17, 2, 18, 16, 12, 13)
+EARLY = (6, 0, 1, 4, 5)
+LATE = (14, 15, 8, 9, 10, 11, 7, 3, 17, 2, 18, 16, 12, 13)
 MESH = pl.DeviceIdType.MESH
 BF16 = jnp.bfloat16
 F32 = jnp.float32
@@ -202,7 +203,7 @@
     loads = [
         pltpu.make_async_copy(sources[i], held[i], isem.at[i]) for i in range(INPUTS)
     ]
-    for i in ORDER:
+    for i in EARLY:
         loads[i].start()
 
     def need(*which):
@@ -235,10 +236,12 @@
         return jnp.concatenate([r[o + at : o + at + 16, :] for r, o in refs], 0)
 
     fields = [(q_ref, 0), (q_ref, 64), (q_ref, 128), (q_ref, 192), (f_ref, 192)]
-    need(6, 0, 1, 4)
+    need(6)
+    for way in range(2):
+        exps[way] = hot(ex_ref[way : way + 1, :], 512)
+    need(0, 1, 4)
     psend[...] = jnp.broadcast_to(ps_ref[...], psend.shape)
     for way in range(2):
-        exps[way] = hot(ex_ref[way : way + 1, :], 512)
         both = stack(z_trace(fields, way == 0))
         x2[way * 160 : way * 160 + 160, :] = both
         gathered = dot(both, exps[way])
@@ -254,6 +257,9 @@
         copy = remote(psend, table.at[REACH - s], pssem.at[i], prsem.at[REACH - s], s)
         copy.start()
         pcopies.append(copy)
+
+    for i in LATE:
+        loads[i].start()
 
     need(5)
     for f in range(6):
@@ -316,67 +322,78 @@
     spread = dot(stack(block_step), repeat)
     step = jnp.concatenate([spread[:8] + spread[8:]] * 8, 0)
 
+    need(17, 2)
+
+    def advance(first, last, face=None):
+        count = wide(count_ref[first:last, :])
+        size = last - first
+        s_part = sense[first:last]
+        r_a = main[first:last]
+        r_b = main[64 + first : 64 + last] + main_low[first:last]
+        if face is not None:
+            sign, far = face
+            s_part = s_part - HALF * sign * far[64:80]
+            r_a = r_a + HALF * far[0:16]
+            r_b = r_b - HALF * sign * far[48:64]
+        r_b = r_b + 2.0 * step[0:size] * s_part
+        q = q_ref[first:last, :]
+        new = q - count * q + DT * (r_a + bulk[0:size] * r_b)
+        t_out[first:last, :] = new
+        lam_p = a_ref[first:last, :] + new
+        k_lam = bulk[0:size] * lam_p
+        a_out[first:last, :] = lam_p
+        states = [k_lam]
+        for k in range(3):
+            low, high = 64 + 64 * k + first, 64 + 64 * k + last
+            r_u = main[64 + low : 64 + high] + main_low[low:high]
+            if face is not None:
+                add = far[16 + 16 * k : 32 + 16 * k]
+                if k == 2:
+                    add = add - sign * far[0:16]
+                r_u = r_u + HALF * add
+            q = q_ref[low:high, :]
+            new = q - count * q + DT * r_u
+            t_out[low:high, :] = new
+            lam = a_ref[low:high, :] + new
+            a_out[low:high, :] = lam
+            states.append(lam)
+        states.append(lam_p)
+        return states, s_part
+
+    def keep(states, first, last):
+        for i, value in enumerate(states):
+            high, low = split(value)
+            x2[64 * i + first : 64 * i + last, :] = high
+            x2[320 + 64 * i + first : 320 + 64 * i + last, :] = low
+
+    copies2 = []
+    zboth = []
+    ends = []
     for way in range(2):
         copies1[way].wait()
         outside = dot(stack(recv1[way]), ghots[way])
-        wz[way] = wz[way] + outside[:80] + outside[80:]
-
-    low, high = wz[0], wz[1]
+        far = wz[way] + outside[:80] + outside[80:]
+        at = 48 * way
+        states, s_part = advance(at, at + 16, (2.0 * way - 1.0, far))
+        both = stack(jnp.concatenate(states, 0))
+        gathered = dot(both, exps[1 - way])
+        send2[way] = gathered[:80] + gathered[80:]
+        copy = remote(send2.at[way], recv2.at[way], ssem2.at[way], rsem2.at[way], 2 * way - 1)
+        copy.start()
+        copies2.append(copy)
+        zboth.append(both)
+        ends.append((states, s_part))
+    middle = advance(16, 48)
+    for way in range(2):
+        keep(ends[way][0], 48 * way, 48 * way + 16)
+    keep(middle[0], 16, 48)
+    lam_p = jnp.concatenate([ends[0][0][4], middle[0][4], ends[1][0][4]], 0)
+    sense = jnp.concatenate([ends[0][1], middle[1], ends[1][1]], 0)
 
     def z_add(value, first, last):
         return jnp.concatenate([value[0:16] + first, value[16:48], value[48:64] + last], 0)
 
-    sense = z_add(sense, HALF * low[64:80], -HALF * high[64:80])
-    r_a = z_add(main[0:64], HALF * low[0:16], HALF * high[0:16])
-    r_b = z_add(main[64:128] + main_low[0:64], HALF * low[48:64], -HALF * high[48:64])
-    r_b = r_b + 2.0 * step * sense
-    need(17, 2)
     count = wide(count_ref[...])
-    q = q_ref[0:64, :]
-    new = q - count * q + DT * (r_a + bulk * r_b)
-    t_out[0:64, :] = new
-    lam = a_ref[0:64, :] + new
-    lam_p = lam
-    k_lam = bulk * lam
-    a_out[0:64, :] = lam
-    k_h, k_l = split(k_lam)
-    p_h, p_l = split(lam)
-    x2[0:64, :] = k_h
-    x2[320:384, :] = k_l
-    x2[256:320, :] = p_h
-    x2[576:640, :] = p_l
-    ztop = [k_lam[48:64]]
-    zbot = [k_lam[0:16]]
-    for k in range(3):
-        at = 64 + 64 * k
-        first, last = low[16 + 16 * k : 32 + 16 * k], high[16 + 16 * k : 32 + 16 * k]
-        if k == 2:
-            first = first + low[0:16]
-            last = last - high[0:16]
-        r_u = z_add(main[64 + at : 128 + at] + main_low[at : at + 64], HALF * first, HALF * last)
-        q = q_ref[at : at + 64, :]
-        new = q - count * q + DT * r_u
-        t_out[at : at + 64, :] = new
-        lam = a_ref[at : at + 64, :] + new
-        a_out[at : at + 64, :] = lam
-        l_h, l_l = split(lam)
-        x2[at : at + 64, :] = l_h
-        x2[320 + at : 384 + at, :] = l_l
-        ztop.append(lam[48:64])
-        zbot.append(lam[0:16])
-    ztop.append(lam_p[48:64])
-    zbot.append(lam_p[0:16])
-
-    copies2 = []
-    zboth = []
-    for way in range(2):
-        both = stack(jnp.concatenate(ztop if way == 0 else zbot, 0))
-        zboth.append(both)
-        gathered = dot(both, exps[way])
-        send2[way] = gathered[:80] + gathered[80:]
-        copy = remote(send2.at[way], recv2.at[way], ssem2.at[way], rsem2.at[way], 1 - 2 * way)
-        copy.start()
-        copies2.append(copy)
 
     need(18)
     term = bulk * wide(mass_ref[...]) * lam_p * sense
@@ -397,7 +414,7 @@
 
     need(16, 12, 13)
     for way in range(2):
-        inside = dot(zboth[way], hots[4 + way])
+        inside = dot(zboth[1 - way], hots[4 + way])
         wz[way] = inside[:80] + inside[80:]
     t_h = dot(sel_a[...], x2[0:320, :]).astype(BF16)
     t_l = dot(sel_a[...], x2[320:640, :]).astype(BF16)
@@ -411,8 +428,8 @@
 
     for way in range(2):
         copies2[way].wait()
-        outside = dot(stack(recv2[way]), ghots[way])
-        wz[way] = wz[way] + outside[:80] + outside[80:]
+        outside = dot(stack(recv2[way]), ghots[1 - way])
+        wz[1 - way] = wz[1 - way] + outside[:80] + outside[80:]
     low, high = wz[0], wz[1]
     for k in range(4):
         at = 64 * k
@@ -434,6 +451,19 @@
     for i in range(len(steps)):
         total = total + hrecv[i]
     h_out[...] = jnp.sum(total, 0, keepdims=True)
+
+
+def place(t_ref, a_ref, h_ref, t_out, a_out, h_out, t_mid, a_mid, h_mid, isem, osem):
+    ways = ((t_ref, t_mid, t_out), (a_ref, a_mid, a_out), (h_ref, h_mid, h_out))
+    ins = [pltpu.make_async_copy(w[0], w[1], isem.at[i]) for i, w in enumerate(ways)]
+    outs = [pltpu.make_async_copy(w[1], w[2], osem.at[i]) for i, w in enumerate(ways)]
+    for copy in ins:
+        copy.start()
+    for arrived, copy in zip(ins, outs):
+        arrived.wait()
+        copy.start()
+    for copy in outs:
+        copy.wait()
 
 
 def solution(mesh):
@@ -499,6 +529,15 @@
                 collective_id=0, has_side_effects=True, vmem_limit_bytes=62 * 2**20
             ),
         )(*args)
+        outs = (t_out, a_out, h_out)
+        any_space = pl.BlockSpec(memory_space=pl.ANY)
+        t_out, a_out, h_out = pl.pallas_call(
+            place,
+            out_shape=tuple(jax.ShapeDtypeStruct(o.shape, o.dtype) for o in outs),
+            in_specs=[any_space] * 3,
+            out_specs=(any_space,) * 3,
+            scratch_shapes=[pltpu.VMEM(o.shape, o.dtype) for o in outs] + [dma((3,)), dma((3,))],
+        )(*outs)
         return (
             t_out.reshape(4, 64, 512),
             a_out.reshape(4, 64, 512),

time: 24 us -> 22.6 us (0.942)
  local copies, waits for them, and re-layouts: 3.24 us -> 0 us
  Pallas kernels: 19.9 us -> 21.8 us
    unnamed x7 -> x0, local copies, waits for them, and re-layouts: 3.24 us -> none
    pallas_call x0 -> x1, Pallas kernels: none -> 2.06 us  [local(): pl.pallas_call(place, out_shape=tuple((jax.ShapeDtypeStruct(o.shape, o.dt...]
where the time goes in v1:
time: 22.6 us; the launch traced here: 22.5 us
  Pallas kernels  21.8 us (96%)
  between operations  0.64 us (3%)
    pallas_call x1, Pallas kernels, local(): pl.pallas_call(functools.partial(kernel, devices, n_blk), out_shape=(jax....  19.7 us
    pallas_call x1, Pallas kernels, local(): pl.pallas_call(place, out_shape=tuple((jax.ShapeDtypeStruct(o.shape, o.dt...  2.06 us

profile of v1, /device:TPU:0, one launch (start us, length us, event | category | flops | bytes accessed | tf_op | source)
XLA Modules:
  0.0 22.5 jit_solution(9891764008627533652)
XLA Ops:
  0.6 19.7 %shard_map.202 = (f32[256,512]{1,0:T(8,128)}, f32[256,512]{1,0:T(8,128)}, f32[1,128]{1,0:T(1,128)}) custom-call(f32[256,512]{1,0:T(8,128)} %bitcast.9, f32[256,512]{1,0:T(8,128)} %bitcast.10, f32[256,512]{1,0:T(8,128)} %bitcast.11, f32[1,512]{1,0:T(1,128)} %bitcast.12, f32[1,128]{1,0:T(1,128)} %bitcast.13, s32[6,512]{1,0:T(8,128)} %refs_5_.1, ...), custom_call_target="tpu_custom_call" | custom-call | tf_op jit(solution)/shard_map/pallas_call | solution.py:492
  20.4 2.1 %shard_map.203 = (f32[256,512]{1,0:T(8,128)}, f32[256,512]{1,0:T(8,128)}, f32[1,128]{1,0:T(1,128)}) custom-call(f32[256,512]{1,0:T(8,128)} %get-tuple-element.9.t_ref, f32[256,512]{1,0:T(8,128)} %get-tuple-element.10.a_ref, f32[1,128]{1,0:T(1,128)} %get-tuple-element.11.h_ref), custom_call_target="tpu_custom_call" | custom-call | tf_op jit(solution)/shard_map/pallas_call | solution.py:534

commit v2 on v1

--- a/solution.py
+++ b/solution.py
@@ -150,11 +150,13 @@
     *refs,
 ):
     sources, refs = refs[:INPUTS], refs[INPUTS:]
-    t_out, a_out, h_out = refs[:3]
+    t_hbm, a_out, h_out = refs[:3]
     refs = refs[3:]
     held, refs = refs[:INPUTS], refs[INPUTS:]
     (
+    t_out,
     isem,
+    osem,
     hots,
     ghots,
     exps,
@@ -384,6 +386,8 @@
         zboth.append(both)
         ends.append((states, s_part))
     middle = advance(16, 48)
+    leave = pltpu.make_async_copy(t_out, t_hbm, osem)
+    leave.start()
     for way in range(2):
         keep(ends[way][0], 48 * way, 48 * way + 16)
     keep(middle[0], 16, 48)
@@ -451,6 +455,7 @@
     for i in range(len(steps)):
         total = total + hrecv[i]
     h_out[...] = jnp.sum(total, 0, keepdims=True)
+    leave.wait()
 
 
 def place(t_ref, a_ref, h_ref, t_out, a_out, h_out, t_mid, a_mid, h_mid, isem, osem):
@@ -497,10 +502,12 @@
                 jax.ShapeDtypeStruct((1, cells), F32),
             ),
             in_specs=[hbm] * INPUTS,
-            out_specs=(vmem,) * 3,
+            out_specs=(hbm, vmem, vmem),
             scratch_shapes=[pltpu.VMEM(a.shape, a.dtype) for a in args]
             + [
+                pltpu.VMEM((256, 512), F32),
                 dma((INPUTS,)),
+                dma(()),
                 pltpu.VMEM((6, 512, 512), BF16),
                 pltpu.VMEM((2, 256, 512), BF16),
                 pltpu.VMEM((2, 512, 256), BF16),

time: 22.6 us -> 22.5 us (level)
  no operation moved by 1% of the time
where the time goes in v2:
time: 22.5 us; the launch traced here: 22.3 us
  Pallas kernels  21.6 us (96%)
  between operations  0.64 us (3%)
    pallas_call x1, Pallas kernels, local(): pl.pallas_call(functools.partial(kernel, devices, n_blk), out_shape=(jax....  19.6 us
    pallas_call x1, Pallas kernels, local(): pl.pallas_call(place, out_shape=tuple((jax.ShapeDtypeStruct(o.shape, o.dt...  2.06 us

profile of v2, /device:TPU:0, one launch (start us, length us, event | category | flops | bytes accessed | tf_op | source)
XLA Modules:
  0.0 22.3 jit_solution(4347358211088400244)
XLA Ops:
  0.6 19.6 %shard_map.202 = (f32[256,512]{1,0:T(8,128)}, f32[256,512]{1,0:T(8,128)}, f32[1,128]{1,0:T(1,128)}) custom-call(f32[256,512]{1,0:T(8,128)} %bitcast.9, f32[256,512]{1,0:T(8,128)} %bitcast.10, f32[256,512]{1,0:T(8,128)} %bitcast.11, f32[1,512]{1,0:T(1,128)} %bitcast.12, f32[1,128]{1,0:T(1,128)} %bitcast.13, s32[6,512]{1,0:T(8,128)} %refs_5_.1, ...), custom_call_target="tpu_custom_call" | custom-call | tf_op jit(solution)/shard_map/pallas_call | solution.py:497
  20.2 2.1 %shard_map.203 = (f32[256,512]{1,0:T(8,128)}, f32[256,512]{1,0:T(8,128)}, f32[1,128]{1,0:T(1,128)}) custom-call(f32[256,512]{1,0:T(8,128)} %get-tuple-element.9.t_ref, f32[256,512]{1,0:T(8,128)} %get-tuple-element.10.a_ref, f32[1,128]{1,0:T(1,128)} %get-tuple-element.11.h_ref), custom_call_target="tpu_custom_call" | custom-call | tf_op jit(solution)/shard_map/pallas_call | solution.py:541
